TPU v7x, 32 devices: a whole 2x2x4 slice. The times are simulated.
32 devices in a mesh: dom: 2 (over y), slab: 16 (over z, x, core).
Axes of the slice: x: 2, y: 2, z: 4, core: 2. Of those that a mesh axis runs over, the one named last changes fastest.
Arguments:
- weights: bfloat16 [16, 64, 64, 128], P('slab', 'dom'), may hold values from 0 to 0.049804688
- moments: bfloat16 [16, 64, 10, 128], P('slab', 'dom'), may hold values from -6 to 6
- block_tile: int32 [16, 64], P('slab', 'dom'), may hold values from 0 to 63, as said below
- block_slab: int32 [16, 64], P('slab', 'dom'), may hold values from 0 to 15, as said below
- block_count: int32 [16, 2], P('slab', 'dom'), may hold values from 8 to 32, as said below
Outputs:
- filtered: float32 [10, 32, 16, 128], P(None, 'slab', 'dom')
Inputs may be any that keep to these rules, and one draw needn't show every extreme that they name: Every device's used blocks are its first block_count slots; in every slab one device uses all 32 slots. `block_slab`: A block's target slab is its own slab or one of the two next to it on the periodic loop. `block_tile`: A block whose target is the next slab names a tile of that slab's first plane (tiles below 32); one whose target is the previous slab a tile of that slab's last plane (tiles from 32).
All inputs are finite; a program needn't handle non-finite values.
Results may differ from a plain program's by a relative error of at most 0.00035.
Values may be sent and summed in bfloat16 or wider, within the bound.
A program may use at most 64 MiB of HBM per device.

v0:
```python
import jax
import jax.numpy as jnp
from jax import lax
from jax.sharding import PartitionSpec as P

SX = 2
RY = 8
NZ = 128


group_blocks = 8
diffusion = 0.16


def passed_along(block, axis, distance):
    devices = range(lax.axis_size(axis))
    route = [((i - distance) % len(devices), i) for i in devices]
    return lax.ppermute(block, axis, route)


def extended_2(block, sides, width, periodic):
    for axis, dim in sides:
        count = lax.axis_size(axis)
        forward = [(i, i + 1) for i in range(count - 1)]
        if periodic:
            forward.append((count - 1, 0))
        backward = [(target, source) for source, target in forward]
        low = lax.ppermute(
            lax.slice_in_dim(block, block.shape[dim] - width, None, axis=dim), axis, forward
        )
        high = lax.ppermute(lax.slice_in_dim(block, 0, width, axis=dim), axis, backward)
        block = jnp.concatenate([low, block, high], axis=dim)
    return block


def smooth_padded(padded):
    center = padded[:, 1:-1, 1:-1]
    zpadded = jnp.pad(center, ((0, 0), (0, 0), (0, 0), (1, 1)))
    adjacent_cell = padded[:, 2:, 1:-1] + padded[:, :-2, 1:-1]
    adjacent_cell = adjacent_cell + padded[:, 1:-1, 2:] + padded[:, 1:-1, :-2]
    adjacent_cell = adjacent_cell + zpadded[:, :, :, 2:] + zpadded[:, :, :, :-2]
    return center + diffusion * (adjacent_cell - 6.0 * center)


def add_group(accum, weight_group, moment_group, tile_grp):
    term_list = jnp.einsum(
        "ixb,iab->ixa", moment_group, weight_group, preferred_element_type=jnp.float32
    )
    term_list = term_list.reshape(term_list.shape[0], term_list.shape[1] * term_list.shape[2])
    term_list = jnp.where((tile_grp >= 0)[:, None], term_list, 0.0)
    return accum.at[jnp.maximum(tile_grp, 0)].add(term_list)


def local(weights, moments, block_tile, block_slab, block_count):
    weight_loc = weights[0]
    moment_loc = moments[0]
    tile_loc = block_tile[0]
    slab_loc = block_slab[0]
    used = block_count[0, 0]
    n_slabs = lax.axis_size("slab")
    n_doms = lax.axis_size("dom")
    my_slab = lax.axis_index("slab")
    slot_total, tile_cells, particles = weight_loc.shape
    moment_count = moment_loc.shape[1]
    rows_all = RY * n_doms
    z_tiles = NZ // tile_cells
    plane_tiles = rows_all * z_tiles
    offset = jnp.mod(slab_loc - my_slab + 1, n_slabs) - 1
    ext_tile = jnp.where(
        offset == 0,
        tile_loc + plane_tiles,
        jnp.where(
            offset == 1, tile_loc + (SX + 1) * plane_tiles, tile_loc - (SX - 1) * plane_tiles
        ),
    )
    slot_ids = jnp.arange(slot_total, dtype=jnp.int32)
    ext_tile = jnp.where(slot_ids < used, ext_tile, -1)
    accum = jnp.zeros(((SX + 2) * plane_tiles, moment_count * tile_cells), jnp.float32)
    group_steps = (used + group_blocks - 1) // group_blocks

    def local_step(step_index, accum_now):
        first = step_index * group_blocks
        weight_group = lax.dynamic_slice_in_dim(weight_loc, first, group_blocks, 0)
        moment_group = lax.dynamic_slice_in_dim(moment_loc, first, group_blocks, 0)
        tile_grp = lax.dynamic_slice_in_dim(ext_tile, first, group_blocks, 0)
        return add_group(accum_now, weight_group, moment_group, tile_grp)

    accum = lax.fori_loop(0, group_steps, local_step, accum)
    extended = accum.reshape(SX + 2, rows_all, z_tiles, moment_count, tile_cells)
    extended = extended.transpose(3, 0, 1, 2, 4).reshape(moment_count, SX + 2, rows_all, NZ)
    from_next = passed_along(extended[:, 0], "slab", -1)
    from_prev = passed_along(extended[:, SX + 1], "slab", 1)
    summed = extended[:, 1 : SX + 1]
    summed = summed.at[:, SX - 1].add(from_next)
    summed = summed.at[:, 0].add(from_prev)
    owned = lax.psum_scatter(summed, "dom", scatter_dimension=2, tiled=True)
    result = owned
    for pass_number in range(2):
        padded = extended_2(result, (("slab", 1),), 1, True)
        padded = extended_2(padded, (("dom", 2),), 1, False)
        result = smooth_padded(padded)
    return result


def solution(mesh):
    return jax.shard_map(
        local,
        mesh=mesh,
        in_specs=(
            P("slab", "dom", None, None),
            P("slab", "dom", None, None),
            P("slab", "dom"),
            P("slab", "dom"),
            P("slab", "dom"),
        ),
        out_specs=P(None, "slab", "dom", None),
        check_vma=False,
    )
```

profile of v0, /device:TPU:0, one launch (start us, length us, event | category | flops | bytes accessed | tf_op | source)
XLA Modules:
  0.0 75.1 jit_solution(8092810279022473382)
XLA Ops:
  7.2 0.9 %copy.23 = bf16[1,32,10,128]{3,2,1,0:T(8,128)(2,1)S(1)} copy(bf16[1,32,10,128]{3,1,2,0:T(8,128)(2,1)} %param.12) | data formatting | bytes 163840 | tf_op args[1]
  8.9 8.8 %while.12 = (s32[]{:T(128)}, f32[128,640]{1,0:T(8,128)S(1)}, s32[]{:T(128)}, s32[32]{0:T(128)S(1)}, bf16[32,10,128]{2,1,0:T(8,128)(2,1)S(1)}, /*index=5*/bf16[32...) while((s32[]{:T(128)}, f32[128,640]{1,0:T(8,128)S(1)}, ...), condition=%wide.region_2.3_spmd, body=%wide.region_0.2_spmd.sunk | while | flops 1320982 | bytes 575247 | solution.py:88
  9.1 1.1 %fusion.39 = f32[8,10,64]{2,1,0:T(8,128)S(1)} fusion(bf16[32,64,128]{2,1,0:T(8,128)(2,1)} %get-tuple-element.150, s32[]{:T(128)S(6)} %select_n.54, bf16[32,10,128]{2,1,0:T(8,128)(2,1)S(1)} %get-tuple-element.149), kind=kOutput, calls=%fused_computation.1.clone.1 | convolution fusion | flops 1310720 | bytes 185344 | tf_op jit(solution)/shard_map/while/body/ixb,iab->ixa/dot_general | solution.py:46
  10.2 0.9 %scatter_custom_fusion.5 = f32[128,640]{1,0:T(8,128)S(1)} fusion(f32[128,640]{1,0:T(8,128)S(1)} %get-tuple-element.135, s32[8]{0:T(128)S(1)} %broadcast_maximum_fusion.2, f32[8,640]{1,0:T(8,128)S(1)} %reshape.112, f32[]{:T(128)} %constant.108.clone.1..sunk, pred[8]{0:T(512)(128)(4,1)S(1)} %broadcast_compare_fusion.2), kind=kCustom, calls=%fused_computation.4.clone.1 | custom fusion | flops 10240 | bytes 348676 | tf_op jit(solution)/shard_map/while/body/scatter-add | solution.py:51
  11.3 1.1 %fusion.39 = f32[8,10,64]{2,1,0:T(8,128)S(1)} fusion(bf16[32,64,128]{2,1,0:T(8,128)(2,1)} %get-tuple-element.150, s32[]{:T(128)S(6)} %select_n.54, bf16[32,10,128]{2,1,0:T(8,128)(2,1)S(1)} %get-tuple-element.149), kind=kOutput, calls=%fused_computation.1.clone.1 | convolution fusion | flops 1310720 | bytes 185344 | tf_op jit(solution)/shard_map/while/body/ixb,iab->ixa/dot_general | solution.py:46
  12.4 0.9 %scatter_custom_fusion.5 = f32[128,640]{1,0:T(8,128)S(1)} fusion(f32[128,640]{1,0:T(8,128)S(1)} %get-tuple-element.135, s32[8]{0:T(128)S(1)} %broadcast_maximum_fusion.2, f32[8,640]{1,0:T(8,128)S(1)} %reshape.112, f32[]{:T(128)} %constant.108.clone.1..sunk, pred[8]{0:T(512)(128)(4,1)S(1)} %broadcast_compare_fusion.2), kind=kCustom, calls=%fused_computation.4.clone.1 | custom fusion | flops 10240 | bytes 348676 | tf_op jit(solution)/shard_map/while/body/scatter-add | solution.py:51
  13.5 1.1 %fusion.39 = f32[8,10,64]{2,1,0:T(8,128)S(1)} fusion(bf16[32,64,128]{2,1,0:T(8,128)(2,1)} %get-tuple-element.150, s32[]{:T(128)S(6)} %select_n.54, bf16[32,10,128]{2,1,0:T(8,128)(2,1)S(1)} %get-tuple-element.149), kind=kOutput, calls=%fused_computation.1.clone.1 | convolution fusion | flops 1310720 | bytes 185344 | tf_op jit(solution)/shard_map/while/body/ixb,iab->ixa/dot_general | solution.py:46
  14.6 0.9 %scatter_custom_fusion.5 = f32[128,640]{1,0:T(8,128)S(1)} fusion(f32[128,640]{1,0:T(8,128)S(1)} %get-tuple-element.135, s32[8]{0:T(128)S(1)} %broadcast_maximum_fusion.2, f32[8,640]{1,0:T(8,128)S(1)} %reshape.112, f32[]{:T(128)} %constant.108.clone.1..sunk, pred[8]{0:T(512)(128)(4,1)S(1)} %broadcast_compare_fusion.2), kind=kCustom, calls=%fused_computation.4.clone.1 | custom fusion | flops 10240 | bytes 348676 | tf_op jit(solution)/shard_map/while/body/scatter-add | solution.py:51
  15.7 1.1 %fusion.39 = f32[8,10,64]{2,1,0:T(8,128)S(1)} fusion(bf16[32,64,128]{2,1,0:T(8,128)(2,1)} %get-tuple-element.150, s32[]{:T(128)S(6)} %select_n.54, bf16[32,10,128]{2,1,0:T(8,128)(2,1)S(1)} %get-tuple-element.149), kind=kOutput, calls=%fused_computation.1.clone.1 | convolution fusion | flops 1310720 | bytes 185344 | tf_op jit(solution)/shard_map/while/body/ixb,iab->ixa/dot_general | solution.py:46
  16.8 0.9 %scatter_custom_fusion.5 = f32[128,640]{1,0:T(8,128)S(1)} fusion(f32[128,640]{1,0:T(8,128)S(1)} %get-tuple-element.135, s32[8]{0:T(128)S(1)} %broadcast_maximum_fusion.2, f32[8,640]{1,0:T(8,128)S(1)} %reshape.112, f32[]{:T(128)} %constant.108.clone.1..sunk, pred[8]{0:T(512)(128)(4,1)S(1)} %broadcast_compare_fusion.2), kind=kCustom, calls=%fused_computation.4.clone.1 | custom fusion | flops 10240 | bytes 348676 | tf_op jit(solution)/shard_map/while/body/scatter-add | solution.py:51
  18.7 1.1 %collective-permute-start = (f32[10,16,128]{2,1,0:T(8,128)S(1)}, f32[10,16,128]{2,1,0:T(8,128)S(1)}, u32[]{:S(2)}, u32[]{:S(2)}) collective-permute-start(f32[10,16,128]{2,1,0:T(8,128)S(1)} %get-tuple-element.76), channel_id=1, source_target_pairs={{1,0},{2,1},{3,2},{4,3},{5,4},{6,5},{7,6},{8,7},{9,8},{10,9},{11,1... | collective-permute-start | bytes 245768 | tf_op jit(solution)/shard_map/ppermute | solution.py:18
  19.8 2.0 %collective-permute-done = f32[10,16,128]{2,1,0:T(8,128)S(1)} collective-permute-done((f32[10,16,128]{2,1,0:T(8,128)S(1)}, f32[10,16,128]{2,1,0:T(8,128)S(1)}, u32[]{:S(2)}, u32[]{:S(2)}) %collective-permute-start) | collective-permute-done | bytes 81952 | tf_op jit(solution)/shard_map/ppermute | solution.py:18
  21.8 4.5 %collective-permute-done.1 = f32[10,16,128]{2,1,0:T(8,128)S(1)} collective-permute-done((f32[10,16,128]{2,1,0:T(8,128)S(1)}, f32[10,16,128]{2,1,0:T(8,128)S(1)}, u32[]{:S(2)}, u32[]{:S(2)}) %collective-permute-start.1) | collective-permute-done | bytes 81952 | tf_op jit(solution)/shard_map/ppermute | solution.py:18
  27.0 12.4 %reduce-scatter.2.cloned.1.call-done = f32[10,2,8,128]{3,2,0,1:T(8,128)} async-done(((f32[10,2,16,128]{3,2,0,1:T(8,128)}), f32[10,2,8,128]{3,2,0,1:T(8,128)}) %reduce-scatter.2.cloned.1.call-update) | async-done | bytes 81936 | tf_op jit(solution)/shard_map/reduce_scatter | solution.py:96
  40.3 4.4 %collective-permute-start.2 = (f32[10,1,8,128]{3,2,0,1:T(8,128)S(1)}, f32[10,1,8,128]{3,2,0,1:T(8,128)S(1)}, u32[]{:S(2)}, u32[]{:S(2)}) collective-permute-start(f32[10,1,8,128]{3,2,0,1:T(8,128)S(1)} %get-tuple-element.83), channel_id=1, source_target_pairs={{1,0},{2,1},{3,2},{4,3},{5,4},{6,5},{7,6},{8,7},{9,8},{10,9},{11,1... | collective-permute-start | bytes 122888 | tf_op jit(solution)/shard_map/ppermute | solution.py:31
  44.7 1.7 %collective-permute-done.3 = f32[10,1,8,128]{3,2,0,1:T(8,128)S(1)} collective-permute-done((f32[10,1,8,128]{3,2,0,1:T(8,128)S(1)}, f32[10,1,8,128]{3,2,0,1:T(8,128)S(1)}, u32[]{:S(2)}, u32[]{:S(2)}) %collective-permute-start.3) | collective-permute-done | bytes 40992 | tf_op jit(solution)/shard_map/ppermute | solution.py:28
  46.5 1.3 %collective-permute-start.4 = (f32[10,4,1,128]{3,2,0,1:T(1,128)S(1)}, f32[10,4,1,128]{3,2,0,1:T(1,128)S(1)}, u32[]{:S(2)}, u32[]{:S(2)}) collective-permute-start(f32[10,4,1,128]{3,2,0,1:T(1,128)S(1)} %get-tuple-element.79), channel_id=1, source_target_pairs={{16,0},{17,1},{18,2},{19,3},{20,4},{21,5},{22,6},{23,7},{24,8},{25... | collective-permute-start | bytes 61448 | tf_op jit(solution)/shard_map/ppermute | solution.py:31
  47.8 4.5 %collective-permute-start.5 = (f32[10,4,1,128]{3,2,0,1:T(1,128)S(1)}, f32[10,4,1,128]{3,2,0,1:T(1,128)S(1)}, u32[]{:S(2)}, u32[]{:S(2)}) collective-permute-start(f32[10,4,1,128]{3,2,0,1:T(1,128)S(1)} %get-tuple-element.80), channel_id=1, source_target_pairs={{0,16},{1,17},{2,18},{3,19},{4,20},{5,21},{6,22},{7,23},{8,24},{9,... | collective-permute-start | bytes 61448 | tf_op jit(solution)/shard_map/ppermute | solution.py:28
  52.4 1.5 %collective-permute-done.5 = f32[10,4,1,128]{3,2,0,1:T(1,128)S(1)} collective-permute-done((f32[10,4,1,128]{3,2,0,1:T(1,128)S(1)}, f32[10,4,1,128]{3,2,0,1:T(1,128)S(1)}, u32[]{:S(2)}, u32[]{:S(2)}) %collective-permute-start.5) | collective-permute-done | bytes 20512 | tf_op jit(solution)/shard_map/ppermute | solution.py:28
  54.0 4.4 %collective-permute-start.6 = (f32[10,1,8,128]{3,2,0,1:T(8,128)S(1)}, f32[10,1,8,128]{3,2,0,1:T(8,128)S(1)}, u32[]{:S(2)}, u32[]{:S(2)}) collective-permute-start(f32[10,1,8,128]{3,2,0,1:T(8,128)S(1)} %get-tuple-element.82), channel_id=1, source_target_pairs={{1,0},{2,1},{3,2},{4,3},{5,4},{6,5},{7,6},{8,7},{9,8},{10,9},{11,1... | collective-permute-start | bytes 122888 | tf_op jit(solution)/shard_map/ppermute | solution.py:31
  58.5 1.7 %collective-permute-done.7 = f32[10,1,8,128]{3,2,0,1:T(8,128)S(1)} collective-permute-done((f32[10,1,8,128]{3,2,0,1:T(8,128)S(1)}, f32[10,1,8,128]{3,2,0,1:T(8,128)S(1)}, u32[]{:S(2)}, u32[]{:S(2)}) %collective-permute-start.7) | collective-permute-done | bytes 40992 | tf_op jit(solution)/shard_map/ppermute | solution.py:28
  60.2 1.3 %collective-permute-start.8 = (f32[10,4,1,128]{3,2,0,1:T(1,128)S(1)}, f32[10,4,1,128]{3,2,0,1:T(1,128)S(1)}, u32[]{:S(2)}, u32[]{:S(2)}) collective-permute-start(f32[10,4,1,128]{3,2,0,1:T(1,128)S(1)} %get-tuple-element.77), channel_id=1, source_target_pairs={{16,0},{17,1},{18,2},{19,3},{20,4},{21,5},{22,6},{23,7},{24,8},{25... | collective-permute-start | bytes 61448 | tf_op jit(solution)/shard_map/ppermute | solution.py:31
  61.5 4.5 %collective-permute-start.9 = (f32[10,4,1,128]{3,2,0,1:T(1,128)S(1)}, f32[10,4,1,128]{3,2,0,1:T(1,128)S(1)}, u32[]{:S(2)}, u32[]{:S(2)}) collective-permute-start(f32[10,4,1,128]{3,2,0,1:T(1,128)S(1)} %get-tuple-element.78), channel_id=1, source_target_pairs={{0,16},{1,17},{2,18},{3,19},{4,20},{5,21},{6,22},{7,23},{8,24},{9,... | collective-permute-start | bytes 61448 | tf_op jit(solution)/shard_map/ppermute | solution.py:28
  66.0 1.5 %collective-permute-done.9 = f32[10,4,1,128]{3,2,0,1:T(1,128)S(1)} collective-permute-done((f32[10,4,1,128]{3,2,0,1:T(1,128)S(1)}, f32[10,4,1,128]{3,2,0,1:T(1,128)S(1)}, u32[]{:S(2)}, u32[]{:S(2)}) %collective-permute-start.9) | collective-permute-done | bytes 20512 | tf_op jit(solution)/shard_map/ppermute | solution.py:28
  (49 shorter events, 5.3 us)
Async XLA Ops:
  6.5 32.9 %reduce-scatter.2.cloned.1.call-start = ((), (), s32[]{:S(2)}) async-start(), calls=%async_computation.1 | async-start | bytes 245760 | tf_op jit(solution)/shard_map/reduce_scatter | solution.py:96
  8.2 0.7 copy-start.2
  8.2 0.7 copy-start.3
  18.7 3.1 %collective-permute-start = (f32[10,16,128]{2,1,0:T(8,128)S(1)}, f32[10,16,128]{2,1,0:T(8,128)S(1)}, u32[]{:S(2)}, u32[]{:S(2)}) collective-permute-start(f32[10,16,128]{2,1,0:T(8,128)S(1)} %get-tuple-element.76), channel_id=1, source_target_pairs={{1,0},{2,1},{3,2},{4,3},{5,4},{6,5},{7,6},{8,7},{9,8},{10,9},{11,1... | collective-permute-start | bytes 245768 | tf_op jit(solution)/shard_map/ppermute | solution.py:18
  19.7 6.6 %collective-permute-start.1 = (f32[10,16,128]{2,1,0:T(8,128)S(1)}, f32[10,16,128]{2,1,0:T(8,128)S(1)}, u32[]{:S(2)}, u32[]{:S(2)}) collective-permute-start(f32[10,16,128]{2,1,0:T(8,128)S(1)} %get-tuple-element.75), channel_id=1, source_target_pairs={{15,0},{0,1},{1,2},{2,3},{3,4},{4,5},{5,6},{6,7},{7,8},{8,9},{9,10... | collective-permute-start | bytes 245768 | tf_op jit(solution)/shard_map/ppermute | solution.py:18
  26.3 0.7 copy-start
  40.3 6.2 %copy-start.1 = (f32[10,2,8,128]{3,2,0,1:T(8,128)S(1)}, f32[10,2,8,128]{3,2,0,1:T(8,128)}, u32[]{:S(2)}) copy-start(f32[10,2,8,128]{3,2,0,1:T(8,128)} %reduce-scatter.2.cloned.1.call-done) | copy-start | bytes 245764
  40.3 6.2 %collective-permute-start.3 = (f32[10,1,8,128]{3,2,0,1:T(8,128)S(1)}, f32[10,1,8,128]{3,2,0,1:T(8,128)S(1)}, u32[]{:S(2)}, u32[]{:S(2)}) collective-permute-start(f32[10,1,8,128]{3,2,0,1:T(8,128)S(1)} %get-tuple-element.84), channel_id=1, source_target_pairs={{0,1},{1,2},{2,3},{3,4},{4,5},{5,6},{6,7},{7,8},{8,9},{9,10},{10,1... | collective-permute-start | bytes 122888 | tf_op jit(solution)/shard_map/ppermute | solution.py:28
  40.3 6.1 %collective-permute-start.2 = (f32[10,1,8,128]{3,2,0,1:T(8,128)S(1)}, f32[10,1,8,128]{3,2,0,1:T(8,128)S(1)}, u32[]{:S(2)}, u32[]{:S(2)}) collective-permute-start(f32[10,1,8,128]{3,2,0,1:T(8,128)S(1)} %get-tuple-element.83), channel_id=1, source_target_pairs={{1,0},{2,1},{3,2},{4,3},{5,4},{6,5},{7,6},{8,7},{9,8},{10,9},{11,1... | collective-permute-start | bytes 122888 | tf_op jit(solution)/shard_map/ppermute | solution.py:31
  46.5 5.9 %collective-permute-start.4 = (f32[10,4,1,128]{3,2,0,1:T(1,128)S(1)}, f32[10,4,1,128]{3,2,0,1:T(1,128)S(1)}, u32[]{:S(2)}, u32[]{:S(2)}) collective-permute-start(f32[10,4,1,128]{3,2,0,1:T(1,128)S(1)} %get-tuple-element.79), channel_id=1, source_target_pairs={{16,0},{17,1},{18,2},{19,3},{20,4},{21,5},{22,6},{23,7},{24,8},{25... | collective-permute-start | bytes 61448 | tf_op jit(solution)/shard_map/ppermute | solution.py:31
  47.8 6.0 %collective-permute-start.5 = (f32[10,4,1,128]{3,2,0,1:T(1,128)S(1)}, f32[10,4,1,128]{3,2,0,1:T(1,128)S(1)}, u32[]{:S(2)}, u32[]{:S(2)}) collective-permute-start(f32[10,4,1,128]{3,2,0,1:T(1,128)S(1)} %get-tuple-element.80), channel_id=1, source_target_pairs={{0,16},{1,17},{2,18},{3,19},{4,20},{5,21},{6,22},{7,23},{8,24},{9,... | collective-permute-start | bytes 61448 | tf_op jit(solution)/shard_map/ppermute | solution.py:28
  54.0 6.2 %collective-permute-start.7 = (f32[10,1,8,128]{3,2,0,1:T(8,128)S(1)}, f32[10,1,8,128]{3,2,0,1:T(8,128)S(1)}, u32[]{:S(2)}, u32[]{:S(2)}) collective-permute-start(f32[10,1,8,128]{3,2,0,1:T(8,128)S(1)} %get-tuple-element.81), channel_id=1, source_target_pairs={{0,1},{1,2},{2,3},{3,4},{4,5},{5,6},{6,7},{7,8},{8,9},{9,10},{10,1... | collective-permute-start | bytes 122888 | tf_op jit(solution)/shard_map/ppermute | solution.py:28
  54.0 6.1 %collective-permute-start.6 = (f32[10,1,8,128]{3,2,0,1:T(8,128)S(1)}, f32[10,1,8,128]{3,2,0,1:T(8,128)S(1)}, u32[]{:S(2)}, u32[]{:S(2)}) collective-permute-start(f32[10,1,8,128]{3,2,0,1:T(8,128)S(1)} %get-tuple-element.82), channel_id=1, source_target_pairs={{1,0},{2,1},{3,2},{4,3},{5,4},{6,5},{7,6},{8,7},{9,8},{10,9},{11,1... | collective-permute-start | bytes 122888 | tf_op jit(solution)/shard_map/ppermute | solution.py:31
  60.2 5.9 %collective-permute-start.8 = (f32[10,4,1,128]{3,2,0,1:T(1,128)S(1)}, f32[10,4,1,128]{3,2,0,1:T(1,128)S(1)}, u32[]{:S(2)}, u32[]{:S(2)}) collective-permute-start(f32[10,4,1,128]{3,2,0,1:T(1,128)S(1)} %get-tuple-element.77), channel_id=1, source_target_pairs={{16,0},{17,1},{18,2},{19,3},{20,4},{21,5},{22,6},{23,7},{24,8},{25... | collective-permute-start | bytes 61448 | tf_op jit(solution)/shard_map/ppermute | solution.py:31
  61.5 6.0 %collective-permute-start.9 = (f32[10,4,1,128]{3,2,0,1:T(1,128)S(1)}, f32[10,4,1,128]{3,2,0,1:T(1,128)S(1)}, u32[]{:S(2)}, u32[]{:S(2)}) collective-permute-start(f32[10,4,1,128]{3,2,0,1:T(1,128)S(1)} %get-tuple-element.78), channel_id=1, source_target_pairs={{0,16},{1,17},{2,18},{3,19},{4,20},{5,21},{6,22},{7,23},{8,24},{9,... | collective-permute-start | bytes 61448 | tf_op jit(solution)/shard_map/ppermute | solution.py:28
Sparse Core Ops, SparseCore 0:
  27.1 12.2 reduce-scatter.1
where the time goes:
time: 75.5 us; the launch traced here: 75.1 us
  waiting for transfers between devices  25.2 us (33%)
  starting transfers between devices  21.7 us (29%)
  between operations  14.3 us (19%)
  local copies, waits for them, and re-layouts  5.15 us (7%)
  other arithmetic  4.36 us (6%)
  matrix products  4.22 us (6%)
    reduce_scatter x1, waiting for transfers between devices, local(): owned = lax.psum_scatter(summed, 'dom', scatter_dimension=2, tiled=True)  12.4 us
    ppermute x4, starting transfers between devices, extended_2(): lax.ppermute(lax.slice_in_dim(block, 0, width, axis=dim), axis, backward)  11.4 us
    ppermute x4, starting transfers between devices, extended_2(): lax.ppermute(lax.slice_in_dim(block, block.shape[dim] - width, None, axis...  9.2 us
    ppermute x2, waiting for transfers between devices, passed_along(): return lax.ppermute(block, axis, route)  6.51 us
    ppermute x4, waiting for transfers between devices, extended_2(): lax.ppermute(lax.slice_in_dim(block, block.shape[dim] - width, None, axis...  6.27 us
    dot_general x4, matrix products, add_group(): jnp.einsum('ixb,iab->ixa', moment_group, weight_group, preferred_element_...  4.22 us
    scatter-add x4, other arithmetic, add_group(): return accum.at[jnp.maximum(tile_grp, 0)].add(term_list)  3.43 us
    unnamed x12, local copies, waits for them, and re-layouts  2.28 us
  transfers between devices with their start and end apart: 11, of which 7 were waited for; matrix products, arithmetic and copies ran while one was open for 0% of the time, Pallas kernels for 0%

commit v1 on v0

v1 whole, which is shorter than its diff:
```python
import functools

import jax
import jax.numpy as jnp
from jax import lax
from jax.experimental import pallas as pl
from jax.experimental.pallas import tpu as pltpu
from jax.sharding import PartitionSpec as P

SX = 2
RY = 8
NZ = 128
SUB = 16
PLANES = 8
diffusion = 0.16
MESH = pl.DeviceIdType.MESH
RANGES = {-2: (0, 1), -1: (1, 3), 0: (3, 5), 1: (5, 7), 2: (7, 8)}
ORDER = (2, -2, 1, -1, 0)


def in_plane(field, rows):
    count = field.shape[0]
    row = lax.broadcasted_iota(jnp.int32, field.shape, 0) % rows
    lane = lax.broadcasted_iota(jnp.int32, field.shape, 1)
    below = jnp.where(row == 0, 0.0, pltpu.roll(field, 1, 0))
    above = jnp.where(row == rows - 1, 0.0, pltpu.roll(field, count - 1, 0))
    left = jnp.where(lane == 0, 0.0, pltpu.roll(field, 1, 1))
    right = jnp.where(lane == NZ - 1, 0.0, pltpu.roll(field, NZ - 1, 1))
    near = (below + above) + (left + right)
    return (1.0 - 6.0 * diffusion) * field + diffusion * near


def two_passes(field, rows):
    once = in_plane(field, rows)
    twice = in_plane(once, rows) + (2.0 * diffusion * diffusion) * field
    planes = []
    for j in range(PLANES):
        e = j - 2
        total = None
        for source, at, factor in (
            (twice, e, 1.0),
            (once, e - 1, 2.0 * diffusion),
            (once, e + 1, 2.0 * diffusion),
            (field, e - 2, diffusion * diffusion),
            (field, e + 2, diffusion * diffusion),
        ):
            if 0 <= at < SX + 2:
                part = factor * source[at * rows : (at + 1) * rows]
                total = part if total is None else total + part
        planes.append(total)
    return planes


def kernel(
    n_doms, n_slabs,
    w_hbm, m_hbm, tile_hbm, slab_hbm, count_hbm, out_ref,
    w_ref, m_ref, tile_ref, slab_ref, count_ref,
    mpad, terms, sbuf, rbuf, load_sem, send_sem, recv_sem,
):
    my_dom = lax.axis_index("dom")
    my_slab = lax.axis_index("slab")
    loads = [
        pltpu.make_async_copy(src, dst, load_sem.at[i])
        for i, (src, dst) in enumerate(
            (
                (m_hbm.at[0], m_ref),
                (w_hbm.at[0], w_ref),
                (tile_hbm, tile_ref),
                (slab_hbm, slab_ref),
                (count_hbm, count_ref),
            )
        )
    ]
    for load in loads:
        load.start()

    peers = [(k, ds) for k in range(n_doms) for ds in ORDER if k or ds]

    def peer(k, ds):
        return (lax.rem(my_dom + k, n_doms), lax.rem(my_slab + ds + n_slabs, n_slabs))

    barrier = pltpu.get_barrier_semaphore()
    for k, ds in peers:
        pl.semaphore_signal(barrier, inc=1, device_id=peer(k, ds), device_id_type=MESH)

    mpad[...] = jnp.zeros_like(mpad)
    for load in loads:
        load.wait()
    blocks, moments, particles = m_ref.shape
    cells = w_ref.shape[1]
    rows = RY * n_doms
    plane_tiles = rows * (NZ // cells)
    half_rows = (SX + 2) * rows
    mpad[:, 0:moments, :] = m_ref[...]

    lane = lax.broadcasted_iota(jnp.int32, (SUB, NZ), 1)
    for j in range(blocks // 4):
        left = mpad[4 * j : 4 * j + 4].reshape(4 * SUB, particles)
        right = w_ref[4 * j : 4 * j + 4].reshape(4 * cells, particles)
        product = lax.dot_general(
            left, right, (((1,), (1,)), ((), ())), preferred_element_type=jnp.float32
        )
        for i in range(4):
            piece = product[SUB * i : SUB * (i + 1), NZ * (i // 2) : NZ * (i // 2 + 1)]
            other = pltpu.roll(piece, NZ // 2, 1)
            low, high = (piece, other) if i % 2 == 0 else (other, piece)
            b = 4 * j + i
            terms[SUB * b : SUB * (b + 1), :] = jnp.where(lane < cells, low, high)

    tile = tile_ref[...]
    step = slab_ref[...] - my_slab
    ahead = jnp.logical_or(step == 1, step == 1 - n_slabs)
    behind = jnp.logical_or(step == -1, step == n_slabs - 1)
    shift = jnp.where(ahead, SX + 1, jnp.where(behind, 1 - SX, 1)) * plane_tiles
    ext = tile + shift
    ext = (ext & 1) * half_rows + (ext >> 1)
    slot = lax.broadcasted_iota(jnp.int32, ext.shape, 1)
    ext = jnp.where(slot < count_ref[...], ext, -1)
    place = lax.broadcasted_iota(jnp.int32, (2 * half_rows, blocks), 0)
    hot = jnp.where(place == ext, 1.0, 0.0).astype(jnp.bfloat16)

    wide = lax.broadcasted_iota(jnp.int32, (half_rows, NZ), 1) < cells
    for m in range(moments):
        term = terms[pl.ds(m, blocks, stride=SUB), :]
        total = None
        for _ in range(3):
            part = term.astype(jnp.bfloat16)
            term = term - part.astype(jnp.float32)
            added = jnp.dot(hot, part, preferred_element_type=jnp.float32)
            total = added if total is None else total + added
        field = jnp.where(wide, total[:half_rows], total[half_rows:])
        planes = two_passes(field, rows)
        for j in range(PLANES):
            for d in range(n_doms):
                sbuf[d, j, m] = planes[j][RY * d : RY * (d + 1)]

    pl.semaphore_wait(barrier, len(peers))
    copies = []
    for n, (k, ds) in enumerate(peers):
        first, last = RANGES[ds]
        target = peer(k, ds)
        copies.append(
            pltpu.make_async_remote_copy(
                src_ref=sbuf.at[target[0], pl.ds(first, last - first)],
                dst_ref=rbuf.at[k, pl.ds(first, last - first)],
                send_sem=send_sem.at[n],
                recv_sem=recv_sem.at[n],
                device_id=target,
                device_id_type=MESH,
            )
        )
    for copy in copies:
        copy.start()
    own = sbuf.at[my_dom]
    even, odd = own[3], own[4]
    for (k, ds), copy in reversed(list(zip(peers, copies))):
        copy.wait_recv()
        first, last = RANGES[ds]
        for j in range(first, last):
            if j % 2:
                even = even + rbuf[k, j]
            else:
                odd = odd + rbuf[k, j]
    out_ref[:, 0] = even
    out_ref[:, 1] = odd
    for copy in copies:
        copy.wait_send()


def local(n_doms, n_slabs, weights, moments, block_tile, block_slab, block_count):
    _, blocks, cells, particles = weights.shape
    mom = moments.shape[2]
    n_peers = 5 * n_doms - 1
    return pl.pallas_call(
        functools.partial(kernel, n_doms, n_slabs),
        out_shape=jax.ShapeDtypeStruct((mom, SX, RY, NZ), jnp.float32),
        in_specs=[pl.BlockSpec(memory_space=pl.ANY)] * 5,
        out_specs=pl.BlockSpec(memory_space=pltpu.VMEM),
        scratch_shapes=[
            pltpu.VMEM((blocks, cells, particles), jnp.bfloat16),
            pltpu.VMEM((blocks, mom, particles), jnp.bfloat16),
            pltpu.VMEM((1, blocks), jnp.int32),
            pltpu.VMEM((1, blocks), jnp.int32),
            pltpu.VMEM((1, 1), jnp.int32),
            pltpu.VMEM((blocks, SUB, particles), jnp.bfloat16),
            pltpu.VMEM((blocks * SUB, NZ), jnp.float32),
            pltpu.VMEM((n_doms, PLANES, mom, RY, NZ), jnp.float32),
            pltpu.VMEM((n_doms, PLANES, mom, RY, NZ), jnp.float32),
            pltpu.SemaphoreType.DMA((5,)),
            pltpu.SemaphoreType.DMA((n_peers,)),
            pltpu.SemaphoreType.DMA((n_peers,)),
        ],
        compiler_params=pltpu.CompilerParams(
            collective_id=0, has_side_effects=True, vmem_limit_bytes=32 * 1024 * 1024
        ),
    )(weights, moments, block_tile, block_slab, block_count)


def solution(mesh):
    return jax.shard_map(
        functools.partial(local, mesh.shape["dom"], mesh.shape["slab"]),
        mesh=mesh,
        in_specs=(
            P("slab", "dom", None, None),
            P("slab", "dom", None, None),
            P("slab", "dom"),
            P("slab", "dom"),
            P("slab", "dom"),
        ),
        out_specs=P(None, "slab", "dom", None),
        check_vma=False,
    )
```

time: 75.5 us -> 18.5 us (0.25)
  waiting for transfers between devices: 25.2 us -> 0 us
  starting transfers between devices: 21.7 us -> 0 us
  Pallas kernels: 0 us -> 14.9 us
  between operations: 14.3 us -> 0.7 us
  other arithmetic: 4.36 us -> 0 us
  matrix products: 4.22 us -> 0 us
  local copies, waits for them, and re-layouts: 5.15 us -> 2.62 us
    ppermute x10 -> x0, starting transfers between devices: 21.7 us -> none  [the longest x4 11.4 us: extended_2(): lax.ppermute(lax.slice_in_dim(block, 0, width, axis=dim), axis, backward)]
    pallas_call x0 -> x1, Pallas kernels: none -> 14.9 us  [local(): pl.pallas_call(functools.partial(kernel, n_doms, n_slabs), out_shape=jax....]
    ppermute x10 -> x0, waiting for transfers between devices: 12.8 us -> none  [the longest x2 6.51 us: passed_along(): return lax.ppermute(block, axis, route)]
    reduce_scatter x1 -> x0, waiting for transfers between devices: 12.4 us -> none  [local(): owned = lax.psum_scatter(summed, 'dom', scatter_dimension=2, tiled=True)]
    dot_general x4 -> x0, matrix products: 4.22 us -> none  [add_group(): jnp.einsum('ixb,iab->ixa', moment_group, weight_group, preferred_element_...]
    scatter-add x6 -> x0, other arithmetic: 3.46 us -> none  [the longest x4 3.43 us: add_group(): return accum.at[jnp.maximum(tile_grp, 0)].add(term_list)]
    reshape x6 -> x0, local copies, waits for them, and re-layouts: 1 us -> none  [the longest x4 0.42 us: add_group(): term_list.reshape(term_list.shape[0], term_list.shape[1] * term_list.shap...]
    slice x4 -> x0, local copies, waits for them, and re-layouts: 0.85 us -> none  [the longest x2 0.83 us: extended_2(): lax.slice_in_dim(block, 0, width, axis=dim)]
  transfers between devices with their start and end apart: 11 -> 0, of which waited for: 7 -> 0; matrix products, arithmetic and copies ran while one was open for 0% -> 0% of each run, Pallas kernels for 0% -> 0%
where the time goes in v1:
time: 18.5 us; the launch traced here: 18.3 us
  Pallas kernels  14.9 us (81%)
  local copies, waits for them, and re-layouts  2.62 us (14%)
  between operations  0.7 us (4%)
    pallas_call x1, Pallas kernels, local(): pl.pallas_call(functools.partial(kernel, n_doms, n_slabs), out_shape=jax....  14.9 us
    unnamed x8, local copies, waits for them, and re-layouts  2.62 us

profile of v1, /device:TPU:0, one launch (start us, length us, event | category | flops | bytes accessed | tf_op | source)
XLA Modules:
  0.0 18.3 jit_solution(9055796917255810158)
XLA Ops:
  0.7 0.0 copy-start.1
  0.7 0.0 copy-start.2
  0.7 0.9 %copy.6.m_hbm = bf16[1,32,10,128]{3,2,1,0:T(8,128)(2,1)S(1)} copy(bf16[1,32,10,128]{3,1,2,0:T(8,128)(2,1)} %param.6) | data formatting | bytes 163840 | tf_op args[1]
  1.6 0.0 copy-done.1
  1.6 0.0 copy-done.2
  1.6 0.0 copy-start
  1.6 1.0 %copy-done = bf16[1,32,64,128]{3,2,1,0:T(8,128)(2,1)S(1)} copy-done((bf16[1,32,64,128]{3,2,1,0:T(8,128)(2,1)S(1)}, bf16[1,32,64,128]{3,2,1,0:T(8,128)(2,1)}, u32[]{:S(2)}) %copy-start) | copy-done | bytes 524312
  2.7 14.9 %shard_map.55 = f32[10,2,8,128]{3,2,1,0:T(8,128)S(1)} custom-call(bf16[1,32,64,128]{3,2,1,0:T(8,128)(2,1)S(1)} %copy-done, bf16[1,32,10,128]{3,2,1,0:T(8,128)(2,1)S(1)} %copy.6.m_hbm, s32[1,32]{1,0:T(1,128)S(1)} %copy-done.1, s32[1,32]{1,0:T(1,128)S(1)} %copy-done.2, s32[1,1]{1,0:T(1,128)S(6)} %copy.8.count_hbm), custom_call_target="tpu_custom_call" | custom-call | tf_op jit(solution)/shard_map/pallas_call | solution.py:174
  17.6 0.6 %copy.9 = f32[10,2,8,128]{3,2,1,0:T(8,128)} copy(f32[10,2,8,128]{3,2,1,0:T(8,128)S(1)} %shard_map.55) | data formatting | bytes 163840
Async XLA Ops:
  0.7 1.0 %copy-start.1 = (s32[1,32]{1,0:T(1,128)S(1)}, s32[1,32]{1,0:T(1,128)}, u32[]{:S(2)}) copy-start(s32[1,32]{1,0:T(1,128)} %tile_hbm.1) | copy-start | bytes 388
  0.7 1.0 %copy-start.2 = (s32[1,32]{1,0:T(1,128)S(1)}, s32[1,32]{1,0:T(1,128)}, u32[]{:S(2)}) copy-start(s32[1,32]{1,0:T(1,128)} %slab_hbm.1) | copy-start | bytes 388
  1.6 1.0 %copy-start = (bf16[1,32,64,128]{3,2,1,0:T(8,128)(2,1)S(1)}, bf16[1,32,64,128]{3,2,1,0:T(8,128)(2,1)}, u32[]{:S(2)}) copy-start(bf16[1,32,64,128]{3,2,1,0:T(8,128)(2,1)} %w_hbm.1) | copy-start | bytes 1572868

commit v2 on v1

--- a/solution.py
+++ b/solution.py
@@ -55,7 +55,7 @@
     n_doms, n_slabs,
     w_hbm, m_hbm, tile_hbm, slab_hbm, count_hbm, out_ref,
     w_ref, m_ref, tile_ref, slab_ref, count_ref,
-    mpad, terms, sbuf, rbuf, load_sem, send_sem, recv_sem,
+    terms, sbuf, rbuf, load_sem, send_sem, recv_sem,
 ):
     my_dom = lax.axis_index("dom")
     my_slab = lax.axis_index("slab")
@@ -83,29 +83,33 @@
     for k, ds in peers:
         pl.semaphore_signal(barrier, inc=1, device_id=peer(k, ds), device_id_type=MESH)
 
-    mpad[...] = jnp.zeros_like(mpad)
     for load in loads:
         load.wait()
-    blocks, moments, particles = m_ref.shape
+    moments, blocks, particles = m_ref.shape
     cells = w_ref.shape[1]
     rows = RY * n_doms
     plane_tiles = rows * (NZ // cells)
     half_rows = (SX + 2) * rows
-    mpad[:, 0:moments, :] = m_ref[...]
-
-    lane = lax.broadcasted_iota(jnp.int32, (SUB, NZ), 1)
-    for j in range(blocks // 4):
-        left = mpad[4 * j : 4 * j + 4].reshape(4 * SUB, particles)
-        right = w_ref[4 * j : 4 * j + 4].reshape(4 * cells, particles)
+
+    row = lax.broadcasted_iota(jnp.int32, (8, NZ), 0)
+    lane = lax.broadcasted_iota(jnp.int32, (8, NZ), 1)
+    in_place = (row % 2 == 0) == (lane < cells)
+    for g in range(blocks // SUB):
+        left = m_ref[:, SUB * g : SUB * (g + 1), :].reshape(moments * SUB, particles)
+        right = w_ref[SUB * g : SUB * (g + 1)].reshape(SUB * cells, particles)
         product = lax.dot_general(
             left, right, (((1,), (1,)), ((), ())), preferred_element_type=jnp.float32
         )
-        for i in range(4):
-            piece = product[SUB * i : SUB * (i + 1), NZ * (i // 2) : NZ * (i // 2 + 1)]
-            other = pltpu.roll(piece, NZ // 2, 1)
-            low, high = (piece, other) if i % 2 == 0 else (other, piece)
-            b = 4 * j + i
-            terms[SUB * b : SUB * (b + 1), :] = jnp.where(lane < cells, low, high)
+        for m in range(moments):
+            for h in range(2):
+                top = SUB * m + 8 * h
+                piece = None
+                for pair in range(4):
+                    at = NZ * (4 * h + pair)
+                    found = product[top : top + 8, at : at + NZ]
+                    piece = found if piece is None else jnp.where(row // 2 == pair, found, piece)
+                both = jnp.where(in_place, piece, pltpu.roll(piece, NZ // 2, 1))
+                terms[m, SUB * g + 8 * h : SUB * g + 8 * (h + 1), :] = both
 
     tile = tile_ref[...]
     step = slab_ref[...] - my_slab
@@ -121,7 +125,7 @@
 
     wide = lax.broadcasted_iota(jnp.int32, (half_rows, NZ), 1) < cells
     for m in range(moments):
-        term = terms[pl.ds(m, blocks, stride=SUB), :]
+        term = terms[m]
         total = None
         for _ in range(3):
             part = term.astype(jnp.bfloat16)
@@ -178,12 +182,11 @@
         out_specs=pl.BlockSpec(memory_space=pltpu.VMEM),
         scratch_shapes=[
             pltpu.VMEM((blocks, cells, particles), jnp.bfloat16),
-            pltpu.VMEM((blocks, mom, particles), jnp.bfloat16),
+            pltpu.VMEM((mom, blocks, particles), jnp.bfloat16),
             pltpu.VMEM((1, blocks), jnp.int32),
             pltpu.VMEM((1, blocks), jnp.int32),
             pltpu.VMEM((1, 1), jnp.int32),
-            pltpu.VMEM((blocks, SUB, particles), jnp.bfloat16),
-            pltpu.VMEM((blocks * SUB, NZ), jnp.float32),
+            pltpu.VMEM((mom, blocks, NZ), jnp.float32),
             pltpu.VMEM((n_doms, PLANES, mom, RY, NZ), jnp.float32),
             pltpu.VMEM((n_doms, PLANES, mom, RY, NZ), jnp.float32),
             pltpu.SemaphoreType.DMA((5,)),
@@ -191,9 +194,9 @@
             pltpu.SemaphoreType.DMA((n_peers,)),
         ],
         compiler_params=pltpu.CompilerParams(
-            collective_id=0, has_side_effects=True, vmem_limit_bytes=32 * 1024 * 1024
+            collective_id=0, has_side_effects=True, vmem_limit_bytes=64 * 1024 * 1024
         ),
-    )(weights, moments, block_tile, block_slab, block_count)
+    )(weights, moments.transpose(0, 2, 1, 3), block_tile, block_slab, block_count)
 
 
 def solution(mesh):

time: 18.5 us -> 17.8 us (0.962)
  local copies, waits for them, and re-layouts: 2.62 us -> 1.53 us
  Pallas kernels: 14.9 us -> 15.4 us
    unnamed x8 -> x1, local copies, waits for them, and re-layouts: 2.62 us -> 1.53 us
    pallas_call x1, Pallas kernels: 14.9 us -> 15.4 us  [local(): pl.pallas_call(functools.partial(kernel, n_doms, n_slabs), out_shape=jax....]
where the time goes in v2:
time: 17.8 us; the launch traced here: 17.6 us
  Pallas kernels  15.4 us (87%)
  local copies, waits for them, and re-layouts  1.53 us (9%)
  between operations  0.66 us (4%)
    pallas_call x1, Pallas kernels, local(): pl.pallas_call(functools.partial(kernel, n_doms, n_slabs), out_shape=jax....  15.4 us
    unnamed x1, local copies, waits for them, and re-layouts  1.53 us

profile of v2, /device:TPU:0, one launch (start us, length us, event | category | flops | bytes accessed | tf_op | source)
XLA Modules:
  0.0 17.6 jit_solution(9905034241329238951)
XLA Ops:
  0.7 15.4 %shard_map.55 = f32[10,2,8,128]{3,2,1,0:T(8,128)} custom-call(bf16[1,32,64,128]{3,2,1,0:T(8,128)(2,1)} %w_hbm.1, bf16[1,10,32,128]{3,2,1,0:T(8,128)(2,1)} %bitcast.1, s32[1,32]{1,0:T(1,128)} %tile_hbm.1, s32[1,32]{1,0:T(1,128)} %slab_hbm.1, s32[1,1]{1,0:T(1,128)S(6)} %copy.7.count_hbm), custom_call_target="tpu_custom_call" | custom-call | tf_op jit(solution)/shard_map/pallas_call | solution.py:178
  16.1 1.5 %copy.8 = f32[10,2,8,128]{3,2,1,0:T(8,128)} copy(f32[10,2,8,128]{3,2,1,0:T(8,128)} %shard_map.55) | data formatting | bytes 163840

commit v3 on v2

--- a/solution.py
+++ b/solution.py
@@ -12,6 +12,8 @@
 NZ = 128
 SUB = 16
 PLANES = 8
+LEVELS = 32766.0
+SMALLEST = 1e-33
 diffusion = 0.16
 MESH = pl.DeviceIdType.MESH
 RANGES = {-2: (0, 1), -1: (1, 3), 0: (3, 5), 1: (5, 7), 2: (7, 8)}
@@ -55,7 +57,8 @@
     n_doms, n_slabs,
     w_hbm, m_hbm, tile_hbm, slab_hbm, count_hbm, out_ref,
     w_ref, m_ref, tile_ref, slab_ref, count_ref,
-    terms, sbuf, rbuf, load_sem, send_sem, recv_sem,
+    terms, fields, peaks, send_scale, send_level, recv_scale, recv_level,
+    load_sem, send_sem, recv_sem,
 ):
     my_dom = lax.axis_index("dom")
     my_slab = lax.axis_index("slab")
@@ -136,45 +139,64 @@
         planes = two_passes(field, rows)
         for j in range(PLANES):
             for d in range(n_doms):
-                sbuf[d, j, m] = planes[j][RY * d : RY * (d + 1)]
-
-    pl.semaphore_wait(barrier, len(peers))
+                block = planes[j][RY * d : RY * (d + 1)]
+                fields[d, j, m] = block
+                peak = jnp.abs(block)
+                peaks[d, j] = peak if m == 0 else jnp.maximum(peaks[d, j], peak)
+
     copies = []
-    for n, (k, ds) in enumerate(peers):
+    for n, ds in enumerate(ORDER):
         first, last = RANGES[ds]
-        target = peer(k, ds)
-        copies.append(
-            pltpu.make_async_remote_copy(
-                src_ref=sbuf.at[target[0], pl.ds(first, last - first)],
-                dst_ref=rbuf.at[k, pl.ds(first, last - first)],
-                send_sem=send_sem.at[n],
-                recv_sem=recv_sem.at[n],
-                device_id=target,
-                device_id_type=MESH,
-            )
-        )
-    for copy in copies:
-        copy.start()
-    own = sbuf.at[my_dom]
-    even, odd = own[3], own[4]
-    for (k, ds), copy in reversed(list(zip(peers, copies))):
-        copy.wait_recv()
-        first, last = RANGES[ds]
-        for j in range(first, last):
-            if j % 2:
-                even = even + rbuf[k, j]
-            else:
-                odd = odd + rbuf[k, j]
-    out_ref[:, 0] = even
-    out_ref[:, 1] = odd
-    for copy in copies:
-        copy.wait_send()
+        for d in range(n_doms):
+            for j in range(first, last):
+                peak = jnp.maximum(jnp.max(peaks[d, j], axis=0, keepdims=True), SMALLEST)
+                send_scale[d, j] = peak * (1.0 / LEVELS)
+                inverse = LEVELS / peak
+                for p in range(moments // 2):
+                    pair = fields[d, j, 2 * p : 2 * p + 2].reshape(2 * RY, NZ)
+                    level = jnp.round(pair * inverse).astype(jnp.int32)
+                    send_level[d, j, p] = level.astype(jnp.int16)
+        if n == 0:
+            pl.semaphore_wait(barrier, len(peers))
+        span = pl.ds(first, last - first)
+        for k in range(n_doms):
+            if k == 0 and ds == 0:
+                continue
+            target = peer(k, ds)
+            group = []
+            for i, (source, landing) in enumerate(
+                ((send_scale, recv_scale), (send_level, recv_level))
+            ):
+                copy = pltpu.make_async_remote_copy(
+                    src_ref=source.at[target[0], span],
+                    dst_ref=landing.at[k, span],
+                    send_sem=send_sem.at[i, k, n],
+                    recv_sem=recv_sem.at[i, k, n],
+                    device_id=target,
+                    device_id_type=MESH,
+                )
+                copy.start()
+                group.append(copy)
+            copies.append((k, ds, group))
+
+    own = fields.at[my_dom]
+    sums = [own[4], own[3]]
+    for k, ds, group in reversed(copies):
+        for copy in group:
+            copy.wait_recv()
+        for j in range(*RANGES[ds]):
+            level = recv_level[k, j].astype(jnp.float32).reshape(moments, RY, NZ)
+            sums[j % 2] = sums[j % 2] + level * recv_scale[k, j]
+    out_ref[:, 0] = sums[1]
+    out_ref[:, 1] = sums[0]
+    for _, _, group in copies:
+        for copy in group:
+            copy.wait_send()
 
 
 def local(n_doms, n_slabs, weights, moments, block_tile, block_slab, block_count):
     _, blocks, cells, particles = weights.shape
     mom = moments.shape[2]
-    n_peers = 5 * n_doms - 1
     return pl.pallas_call(
         functools.partial(kernel, n_doms, n_slabs),
         out_shape=jax.ShapeDtypeStruct((mom, SX, RY, NZ), jnp.float32),
@@ -188,10 +210,14 @@
             pltpu.VMEM((1, 1), jnp.int32),
             pltpu.VMEM((mom, blocks, NZ), jnp.float32),
             pltpu.VMEM((n_doms, PLANES, mom, RY, NZ), jnp.float32),
-            pltpu.VMEM((n_doms, PLANES, mom, RY, NZ), jnp.float32),
+            pltpu.VMEM((n_doms, PLANES, RY, NZ), jnp.float32),
+            pltpu.VMEM((n_doms, PLANES, 1, NZ), jnp.float32),
+            pltpu.VMEM((n_doms, PLANES, mom // 2, 2 * RY, NZ), jnp.int16),
+            pltpu.VMEM((n_doms, PLANES, 1, NZ), jnp.float32),
+            pltpu.VMEM((n_doms, PLANES, mom // 2, 2 * RY, NZ), jnp.int16),
             pltpu.SemaphoreType.DMA((5,)),
-            pltpu.SemaphoreType.DMA((n_peers,)),
-            pltpu.SemaphoreType.DMA((n_peers,)),
+            pltpu.SemaphoreType.DMA((2, n_doms, len(ORDER))),
+            pltpu.SemaphoreType.DMA((2, n_doms, len(ORDER))),
         ],
         compiler_params=pltpu.CompilerParams(
             collective_id=0, has_side_effects=True, vmem_limit_bytes=64 * 1024 * 1024

time: 17.8 us -> 15.1 us (0.85)
  Pallas kernels: 15.4 us -> 12.7 us
    pallas_call x1, Pallas kernels: 15.4 us -> 12.7 us  [local(): pl.pallas_call(functools.partial(kernel, n_doms, n_slabs), out_shape=jax....]
where the time goes in v3:
time: 15.1 us; the launch traced here: 14.9 us
  Pallas kernels  12.7 us (84%)
  local copies, waits for them, and re-layouts  1.53 us (10%)
  between operations  0.66 us (4%)
    pallas_call x1, Pallas kernels, local(): pl.pallas_call(functools.partial(kernel, n_doms, n_slabs), out_shape=jax....  12.7 us
    unnamed x1, local copies, waits for them, and re-layouts  1.53 us

profile of v3, /device:TPU:0, one launch (start us, length us, event | category | flops | bytes accessed | tf_op | source)
XLA Modules:
  0.0 14.9 jit_solution(412409516754980894)
XLA Ops:
  0.7 12.7 %shard_map.55 = f32[10,2,8,128]{3,2,1,0:T(8,128)} custom-call(bf16[1,32,64,128]{3,2,1,0:T(8,128)(2,1)} %w_hbm.1, bf16[1,10,32,128]{3,2,1,0:T(8,128)(2,1)} %bitcast.1, s32[1,32]{1,0:T(1,128)} %tile_hbm.1, s32[1,32]{1,0:T(1,128)} %slab_hbm.1, s32[1,1]{1,0:T(1,128)S(6)} %copy.7.count_hbm), custom_call_target="tpu_custom_call" | custom-call | tf_op jit(solution)/shard_map/pallas_call | solution.py:200
  13.4 1.5 %copy.8 = f32[10,2,8,128]{3,2,1,0:T(8,128)} copy(f32[10,2,8,128]{3,2,1,0:T(8,128)} %shard_map.55) | data formatting | bytes 163840

commit v4 on v3

--- a/solution.py
+++ b/solution.py
@@ -12,6 +12,7 @@
 NZ = 128
 SUB = 16
 PLANES = 8
+LOADS = 4
 LEVELS = 32766.0
 SMALLEST = 1e-33
 diffusion = 0.16
@@ -62,17 +63,14 @@
 ):
     my_dom = lax.axis_index("dom")
     my_slab = lax.axis_index("slab")
+    moments, blocks, particles = m_ref.shape
+    cells = w_ref.shape[1]
+    pairs = [(tile_hbm, tile_ref), (slab_hbm, slab_ref), (count_hbm, count_ref), (m_hbm.at[0], m_ref)]
+    for g in range(LOADS):
+        part = pl.ds(g * (blocks // LOADS), blocks // LOADS)
+        pairs.append((w_hbm.at[0, part], w_ref.at[part]))
     loads = [
-        pltpu.make_async_copy(src, dst, load_sem.at[i])
-        for i, (src, dst) in enumerate(
-            (
-                (m_hbm.at[0], m_ref),
-                (w_hbm.at[0], w_ref),
-                (tile_hbm, tile_ref),
-                (slab_hbm, slab_ref),
-                (count_hbm, count_ref),
-            )
-        )
+        pltpu.make_async_copy(src, dst, load_sem.at[i]) for i, (src, dst) in enumerate(pairs)
     ]
     for load in loads:
         load.start()
@@ -86,18 +84,32 @@
     for k, ds in peers:
         pl.semaphore_signal(barrier, inc=1, device_id=peer(k, ds), device_id_type=MESH)
 
-    for load in loads:
+    for load in loads[:3]:
         load.wait()
-    moments, blocks, particles = m_ref.shape
-    cells = w_ref.shape[1]
     rows = RY * n_doms
     plane_tiles = rows * (NZ // cells)
     half_rows = (SX + 2) * rows
 
+    tile = tile_ref[...]
+    step = slab_ref[...] - my_slab
+    ahead = jnp.logical_or(step == 1, step == 1 - n_slabs)
+    behind = jnp.logical_or(step == -1, step == n_slabs - 1)
+    shift = jnp.where(ahead, SX + 1, jnp.where(behind, 1 - SX, 1)) * plane_tiles
+    ext = tile + shift
+    ext = (ext & 1) * half_rows + (ext >> 1)
+    slot = lax.broadcasted_iota(jnp.int32, ext.shape, 1)
+    ext = jnp.where(slot < count_ref[...], ext, -1)
+    place = lax.broadcasted_iota(jnp.int32, (2 * half_rows, blocks), 0)
+    hot = jnp.where(place == ext, 1.0, 0.0).astype(jnp.bfloat16)
+
     row = lax.broadcasted_iota(jnp.int32, (8, NZ), 0)
     lane = lax.broadcasted_iota(jnp.int32, (8, NZ), 1)
     in_place = (row % 2 == 0) == (lane < cells)
+    loads[3].wait()
     for g in range(blocks // SUB):
+        share = LOADS * SUB // blocks
+        for load in loads[4 + share * g : 4 + share * (g + 1)]:
+            load.wait()
         left = m_ref[:, SUB * g : SUB * (g + 1), :].reshape(moments * SUB, particles)
         right = w_ref[SUB * g : SUB * (g + 1)].reshape(SUB * cells, particles)
         product = lax.dot_general(
@@ -114,23 +126,11 @@
                 both = jnp.where(in_place, piece, pltpu.roll(piece, NZ // 2, 1))
                 terms[m, SUB * g + 8 * h : SUB * g + 8 * (h + 1), :] = both
 
-    tile = tile_ref[...]
-    step = slab_ref[...] - my_slab
-    ahead = jnp.logical_or(step == 1, step == 1 - n_slabs)
-    behind = jnp.logical_or(step == -1, step == n_slabs - 1)
-    shift = jnp.where(ahead, SX + 1, jnp.where(behind, 1 - SX, 1)) * plane_tiles
-    ext = tile + shift
-    ext = (ext & 1) * half_rows + (ext >> 1)
-    slot = lax.broadcasted_iota(jnp.int32, ext.shape, 1)
-    ext = jnp.where(slot < count_ref[...], ext, -1)
-    place = lax.broadcasted_iota(jnp.int32, (2 * half_rows, blocks), 0)
-    hot = jnp.where(place == ext, 1.0, 0.0).astype(jnp.bfloat16)
-
     wide = lax.broadcasted_iota(jnp.int32, (half_rows, NZ), 1) < cells
     for m in range(moments):
         term = terms[m]
         total = None
-        for _ in range(3):
+        for _ in range(2):
             part = term.astype(jnp.bfloat16)
             term = term - part.astype(jnp.float32)
             added = jnp.dot(hot, part, preferred_element_type=jnp.float32)
@@ -215,12 +215,12 @@
             pltpu.VMEM((n_doms, PLANES, mom // 2, 2 * RY, NZ), jnp.int16),
             pltpu.VMEM((n_doms, PLANES, 1, NZ), jnp.float32),
             pltpu.VMEM((n_doms, PLANES, mom // 2, 2 * RY, NZ), jnp.int16),
-            pltpu.SemaphoreType.DMA((5,)),
+            pltpu.SemaphoreType.DMA((4 + LOADS,)),
             pltpu.SemaphoreType.DMA((2, n_doms, len(ORDER))),
             pltpu.SemaphoreType.DMA((2, n_doms, len(ORDER))),
         ],
         compiler_params=pltpu.CompilerParams(
-            collective_id=0, has_side_effects=True, vmem_limit_bytes=64 * 1024 * 1024
+            collective_id=0, has_side_effects=True, vmem_limit_bytes=64 * 1024 * 1024 - 10432 * 1024
         ),
     )(weights, moments.transpose(0, 2, 1, 3), block_tile, block_slab, block_count)
 

time: 15.1 us -> 14.3 us (0.947)
  Pallas kernels: 12.7 us -> 12.2 us
  local copies, waits for them, and re-layouts: 1.53 us -> 1.29 us
    pallas_call x1, Pallas kernels: 12.7 us -> 12.2 us  [local(): pl.pallas_call(functools.partial(kernel, n_doms, n_slabs), out_shape=jax....]
    unnamed x1 -> x5, local copies, waits for them, and re-layouts: 1.53 us -> 1.29 us
where the time goes in v4:
time: 14.3 us; the launch traced here: 14.2 us
  Pallas kernels  12.2 us (85%)
  local copies, waits for them, and re-layouts  1.29 us (9%)
  between operations  0.68 us (5%)
    pallas_call x1, Pallas kernels, local(): pl.pallas_call(functools.partial(kernel, n_doms, n_slabs), out_shape=jax....  12.2 us
    unnamed x5, local copies, waits for them, and re-layouts  1.29 us

profile of v4, /device:TPU:0, one launch (start us, length us, event | category | flops | bytes accessed | tf_op | source)
XLA Modules:
  0.0 14.2 jit_solution(666170404729384720)
XLA Ops:
  0.7 0.0 copy-start
  0.7 0.0 copy-start.1
  0.7 0.6 %copy-done = s32[1,32]{1,0:T(1,128)S(1)} copy-done((s32[1,32]{1,0:T(1,128)S(1)}, s32[1,32]{1,0:T(1,128)}, u32[]{:S(2)}) %copy-start) | copy-done | bytes 152
  1.3 0.0 copy-done.1
  1.3 12.2 %shard_map.55 = f32[10,2,8,128]{3,2,1,0:T(8,128)S(1)} custom-call(bf16[1,32,64,128]{3,2,1,0:T(8,128)(2,1)} %w_hbm.1, bf16[1,10,32,128]{3,2,1,0:T(8,128)(2,1)} %bitcast.1, s32[1,32]{1,0:T(1,128)S(1)} %copy-done, s32[1,32]{1,0:T(1,128)S(1)} %copy-done.1, s32[1,1]{1,0:T(1,128)S(6)} %copy.7.count_hbm), custom_call_target="tpu_custom_call" | custom-call | tf_op jit(solution)/shard_map/pallas_call | solution.py:200
  13.5 0.6 %copy.8 = f32[10,2,8,128]{3,2,1,0:T(8,128)} copy(f32[10,2,8,128]{3,2,1,0:T(8,128)S(1)} %shard_map.55) | data formatting | bytes 163840
Async XLA Ops:
  0.7 0.7 %copy-start = (s32[1,32]{1,0:T(1,128)S(1)}, s32[1,32]{1,0:T(1,128)}, u32[]{:S(2)}) copy-start(s32[1,32]{1,0:T(1,128)} %tile_hbm.1) | copy-start | bytes 388
  0.7 0.7 %copy-start.1 = (s32[1,32]{1,0:T(1,128)S(1)}, s32[1,32]{1,0:T(1,128)}, u32[]{:S(2)}) copy-start(s32[1,32]{1,0:T(1,128)} %slab_hbm.1) | copy-start | bytes 388

commit v5 on v4

--- a/solution.py
+++ b/solution.py
@@ -159,7 +159,7 @@
         if n == 0:
             pl.semaphore_wait(barrier, len(peers))
         span = pl.ds(first, last - first)
-        for k in range(n_doms):
+        for k in reversed(range(n_doms)):
             if k == 0 and ds == 0:
                 continue
             target = peer(k, ds)

time: 14.3 us -> 13.8 us (0.965)
  Pallas kernels: 12.2 us -> 11.7 us
    pallas_call x1, Pallas kernels: 12.2 us -> 11.7 us  [local(): pl.pallas_call(functools.partial(kernel, n_doms, n_slabs), out_shape=jax....]
where the time goes in v5:
time: 13.8 us; the launch traced here: 13.7 us
  Pallas kernels  11.7 us (85%)
  local copies, waits for them, and re-layouts  1.29 us (9%)
  between operations  0.68 us (5%)
    pallas_call x1, Pallas kernels, local(): pl.pallas_call(functools.partial(kernel, n_doms, n_slabs), out_shape=jax....  11.7 us
    unnamed x5, local copies, waits for them, and re-layouts  1.29 us

profile of v5, /device:TPU:0, one launch (start us, length us, event | category | flops | bytes accessed | tf_op | source)
XLA Modules:
  0.0 13.7 jit_solution(10868933924493535103)
XLA Ops:
  0.7 0.0 copy-start
  0.7 0.0 copy-start.1
  0.7 0.6 %copy-done = s32[1,32]{1,0:T(1,128)S(1)} copy-done((s32[1,32]{1,0:T(1,128)S(1)}, s32[1,32]{1,0:T(1,128)}, u32[]{:S(2)}) %copy-start) | copy-done | bytes 152
  1.3 0.0 copy-done.1
  1.3 11.7 %shard_map.55 = f32[10,2,8,128]{3,2,1,0:T(8,128)S(1)} custom-call(bf16[1,32,64,128]{3,2,1,0:T(8,128)(2,1)} %w_hbm.1, bf16[1,10,32,128]{3,2,1,0:T(8,128)(2,1)} %bitcast.1, s32[1,32]{1,0:T(1,128)S(1)} %copy-done, s32[1,32]{1,0:T(1,128)S(1)} %copy-done.1, s32[1,1]{1,0:T(1,128)S(6)} %copy.7.count_hbm), custom_call_target="tpu_custom_call" | custom-call | tf_op jit(solution)/shard_map/pallas_call | solution.py:200
  13.0 0.6 %copy.8 = f32[10,2,8,128]{3,2,1,0:T(8,128)} copy(f32[10,2,8,128]{3,2,1,0:T(8,128)S(1)} %shard_map.55) | data formatting | bytes 163840
Async XLA Ops:
  0.7 0.7 %copy-start = (s32[1,32]{1,0:T(1,128)S(1)}, s32[1,32]{1,0:T(1,128)}, u32[]{:S(2)}) copy-start(s32[1,32]{1,0:T(1,128)} %tile_hbm.1) | copy-start | bytes 388
  0.7 0.7 %copy-start.1 = (s32[1,32]{1,0:T(1,128)S(1)}, s32[1,32]{1,0:T(1,128)}, u32[]{:S(2)}) copy-start(s32[1,32]{1,0:T(1,128)} %slab_hbm.1) | copy-start | bytes 388

commit v6 on v5

--- a/solution.py
+++ b/solution.py
@@ -18,7 +18,7 @@
 diffusion = 0.16
 MESH = pl.DeviceIdType.MESH
 RANGES = {-2: (0, 1), -1: (1, 3), 0: (3, 5), 1: (5, 7), 2: (7, 8)}
-ORDER = (2, -2, 1, -1, 0)
+ORDER = (0, 2, -2, 1, -1)
 
 
 def in_plane(field, rows):

time: 13.8 us -> 13.8 us (level)
  no operation moved by 1% of the time
where the time goes in v6:
time: 13.8 us; the launch traced here: 13.7 us
  Pallas kernels  11.7 us (85%)
  local copies, waits for them, and re-layouts  1.29 us (9%)
  between operations  0.68 us (5%)
    pallas_call x1, Pallas kernels, local(): pl.pallas_call(functools.partial(kernel, n_doms, n_slabs), out_shape=jax....  11.7 us
    unnamed x5, local copies, waits for them, and re-layouts  1.29 us

profile of v6, /device:TPU:0, one launch (start us, length us, event | category | flops | bytes accessed | tf_op | source)
XLA Modules:
  0.0 13.7 jit_solution(3186358929387958811)
XLA Ops:
  0.7 0.0 copy-start
  0.7 0.0 copy-start.1
  0.7 0.6 %copy-done = s32[1,32]{1,0:T(1,128)S(1)} copy-done((s32[1,32]{1,0:T(1,128)S(1)}, s32[1,32]{1,0:T(1,128)}, u32[]{:S(2)}) %copy-start) | copy-done | bytes 152
  1.3 0.0 copy-done.1
  1.3 11.7 %shard_map.55 = f32[10,2,8,128]{3,2,1,0:T(8,128)S(1)} custom-call(bf16[1,32,64,128]{3,2,1,0:T(8,128)(2,1)} %w_hbm.1, bf16[1,10,32,128]{3,2,1,0:T(8,128)(2,1)} %bitcast.1, s32[1,32]{1,0:T(1,128)S(1)} %copy-done, s32[1,32]{1,0:T(1,128)S(1)} %copy-done.1, s32[1,1]{1,0:T(1,128)S(6)} %copy.7.count_hbm), custom_call_target="tpu_custom_call" | custom-call | tf_op jit(solution)/shard_map/pallas_call | solution.py:200
  13.0 0.6 %copy.8 = f32[10,2,8,128]{3,2,1,0:T(8,128)} copy(f32[10,2,8,128]{3,2,1,0:T(8,128)S(1)} %shard_map.55) | data formatting | bytes 163840
Async XLA Ops:
  0.7 0.7 %copy-start = (s32[1,32]{1,0:T(1,128)S(1)}, s32[1,32]{1,0:T(1,128)}, u32[]{:S(2)}) copy-start(s32[1,32]{1,0:T(1,128)} %tile_hbm.1) | copy-start | bytes 388
  0.7 0.7 %copy-start.1 = (s32[1,32]{1,0:T(1,128)S(1)}, s32[1,32]{1,0:T(1,128)}, u32[]{:S(2)}) copy-start(s32[1,32]{1,0:T(1,128)} %slab_hbm.1) | copy-start | bytes 388
